TPU v7x, 512 devices: a whole 4x4x16 slice. The times are simulated.
512 devices in a mesh: gx: 16 (over z), gy: 32 (over x, y, core).
Axes of the slice: x: 4, y: 4, z: 16, core: 2. Of those that a mesh axis runs over, the one named last changes fastest.
Arguments:
- particles: bfloat16 [32768, 4096], P(('gx', 'gy')), may hold values from -6 to 6
- references: bfloat16 [16, 12, 4096], P('gx'), may hold values from -1 to 1
- slot_class: int32 [16], replicated, may hold values from 0 to 15, each once
- log_prior: float32 [16], replicated, may hold values from -2 to 2
- shift_offsets: int32 [8, 2], replicated, may hold values from -8 to 8
- group_ids: int32 [32768], P(('gx', 'gy')), may hold values from 0 to 127
- ctf_table: float32 [128, 2048], replicated, may hold values from -1 to 1
- noise_power: float32 [2048], replicated, may hold values from 0.5 to 2
Outputs:
- class_sums: float32 [16, 12, 4096], P('gx')
- ctf_power: float32 [16, 2048], P('gx')
- log_evidence: float32 [], replicated
Inputs may be any that keep to these rules, and one draw needn't show every extreme that they name: `slot_class`: each class id stands at exactly one slot.
All inputs are finite; a program needn't handle non-finite values.
Results may differ from a plain program's by a relative error of at most 0.006.
Values may be sent and summed in bfloat16 or wider, within the bound.
A program may use at most 64 MiB of HBM per device.

v0:
```python
import functools
import jax
import jax.numpy as jnp
from jax import lax
from jax.sharding import Mesh
from jax.sharding import PartitionSpec as P

L = 64
R = 12
NS = 8
G = 128
HALF = 2048
FR = 4096
GY = ("gy_0", "gy_1", "gy_2")
GX_GY = ("gx", "gy_0", "gy_1", "gy_2")


def in_blocks(shard, dim, length):
    before, after = (shard.shape[:dim], shard.shape[dim + 1 :])
    return jnp.moveaxis(shard.reshape(*before, length, -1, *after), dim, 0)


def summed_on_arrival(shard, axis, dim):
    tiles = in_blocks(shard, dim, lax.axis_size(axis))
    arrived = lax.all_to_all(tiles, axis, split_axis=0, concat_axis=0, tiled=True)
    return arrived.sum(axis=0)


def gathered_total(shard, axis):
    return lax.all_gather(shard, axis).sum(0)


def over_axes(shard, axes):
    return functools.reduce(lax.psum, axes, shard)


def phase_tables(shift_offsets, edge_len):
    half_size = edge_len * edge_len // 2
    freq_index = jnp.arange(half_size, dtype=jnp.int32)
    row_freq = freq_index // (edge_len // 2)
    col_freq = freq_index % (edge_len // 2)
    phase_turns = jnp.mod(
        row_freq[None, :] * shift_offsets[:, 0:1] + col_freq[None, :] * shift_offsets[:, 1:2],
        edge_len,
    )
    angles = phase_turns.astype(jnp.float32) * (2.0 * jnp.pi / edge_len)
    return (jnp.cos(angles), jnp.sin(angles))


def spectra(particles, edge_len):
    rows_here = particles.shape[0]
    half_side = edge_len // 2
    images = particles.astype(jnp.float32).reshape(rows_here * edge_len, edge_len)
    pixel_index = jnp.arange(edge_len, dtype=jnp.int32)
    column_turns = jnp.mod(pixel_index[:, None] * pixel_index[None, :half_side], edge_len).astype(
        jnp.float32
    ) * (2.0 * jnp.pi / edge_len)
    column_table = jnp.concatenate([jnp.cos(column_turns), -jnp.sin(column_turns)], axis=1)
    partial_x = jnp.dot(
        images, column_table, precision=lax.Precision.HIGHEST, preferred_element_type=jnp.float32
    )
    partial_x = partial_x.reshape(rows_here, edge_len, edge_len)
    row_turns = jnp.mod(pixel_index[:, None] * pixel_index[None, :], edge_len).astype(
        jnp.float32
    ) * (2.0 * jnp.pi / edge_len)
    with_cos = jnp.einsum(
        "uy,pyw->puw", jnp.cos(row_turns), partial_x, precision=lax.Precision.HIGHEST
    )
    with_sin = jnp.einsum(
        "uy,pyw->puw", jnp.sin(row_turns), partial_x, precision=lax.Precision.HIGHEST
    )
    real_part = (with_cos[..., :half_side] + with_sin[..., half_side:]) / edge_len
    imag_part = (with_cos[..., half_side:] - with_sin[..., :half_side]) / edge_len
    return (real_part.reshape(rows_here, -1), imag_part.reshape(rows_here, -1))


def shards(
    particles, references, slot_class, log_prior, shift_offsets, group_ids, ctf_table, noise_power
):
    rows_here = particles.shape[0]
    classes = lax.axis_size("gx") * references.shape[0]
    row_width = R * NS
    real_part, imag_part = spectra(particles, L)
    inv_noise = 1.0 / noise_power
    group_hot = (group_ids[:, None] == jnp.arange(G, dtype=jnp.int32)[None, :]).astype(jnp.float32)
    ctf_rows = jnp.dot(
        group_hot, ctf_table, precision=lax.Precision.HIGHEST, preferred_element_type=jnp.float32
    )
    whiten = ctf_rows * inv_noise
    weighted = jnp.concatenate([real_part * whiten, imag_part * whiten], axis=1).astype(
        jnp.bfloat16
    )
    data_power = jnp.sum((real_part * real_part + imag_part * imag_part) * inv_noise, axis=1)
    cosines, sine_table = phase_tables(shift_offsets, L)
    power_table = ctf_table * ctf_table * inv_noise
    blank = jnp.zeros((rows_here, classes * row_width), jnp.float32)
    piece = lax.all_gather(references, "gx", axis=0, tiled=True)

    def add_class(offset, table):
        stack_row = lax.dynamic_index_in_dim(piece, offset, 0, keepdims=False).astype(jnp.float32)
        stack_real = stack_row[:, :HALF]
        stack_imag = stack_row[:, HALF:]
        shifted_real = (
            stack_real[:, None, :] * cosines[None] + stack_imag[:, None, :] * sine_table[None]
        )
        shifted_imag = (
            stack_imag[:, None, :] * cosines[None] - stack_real[:, None, :] * sine_table[None]
        )
        shifted = (
            jnp.concatenate([shifted_real, shifted_imag], axis=2)
            .astype(jnp.bfloat16)
            .reshape(row_width, FR)
        )
        intersection = lax.dot_general(
            weighted, shifted, (((1,), (1,)), ((), ())), preferred_element_type=jnp.float32
        )
        amplitude = stack_real * stack_real + stack_imag * stack_imag
        ref_power = jnp.dot(
            power_table,
            amplitude.T,
            precision=lax.Precision.HIGHEST,
            preferred_element_type=jnp.float32,
        )
        own_power = jnp.dot(
            group_hot,
            ref_power,
            precision=lax.Precision.HIGHEST,
            preferred_element_type=jnp.float32,
        )
        logits = intersection.reshape(rows_here, R, NS) - 0.5 * own_power[:, :, None]
        return lax.dynamic_update_slice_in_dim(
            table, logits.reshape(rows_here, row_width), offset * row_width, 1
        )

    scores = lax.fori_loop(0, piece.shape[0], add_class, blank)
    slot_prior = jnp.sum(
        jnp.where(
            slot_class[:, None] == jnp.arange(classes, dtype=jnp.int32)[None, :],
            log_prior[None, :],
            0.0,
        ),
        axis=1,
    )
    logits = (
        scores.reshape(rows_here, classes, row_width)
        - 0.5 * data_power[:, None, None]
        + slot_prior[None, :, None]
    )
    row_max = jnp.max(logits, axis=(1, 2), keepdims=True)
    raised = jnp.exp(logits - row_max)
    normaliser = jnp.sum(raised, axis=(1, 2), keepdims=True)
    weights = raised / normaliser
    evidence = row_max[:, 0, 0] + jnp.log(normaliser[:, 0, 0])
    weights_low = weights.astype(jnp.bfloat16)
    group_weights = jnp.dot(
        jnp.sum(weights, axis=2).T,
        group_hot,
        precision=lax.Precision.HIGHEST,
        preferred_element_type=jnp.float32,
    )

    def class_terms(slot_index):
        weight_cols = lax.dynamic_index_in_dim(weights_low, slot_index, 1, keepdims=False)
        moment = lax.dot_general(
            weight_cols, weighted, (((0,), (0,)), ((), ())), preferred_element_type=jnp.float32
        )
        moment = moment.reshape(R, NS, FR)
        moment_real = moment[..., :HALF]
        moment_imag = moment[..., HALF:]
        back_real = jnp.sum(moment_real * cosines[None] - moment_imag * sine_table[None], axis=1)
        back_imag = jnp.sum(moment_imag * cosines[None] + moment_real * sine_table[None], axis=1)
        return jnp.concatenate([back_real, back_imag], axis=1)

    owned = summed_on_arrival(
        lax.map(
            lambda offset: class_terms(offset),
            jnp.arange(references.shape[0] * lax.axis_size("gx"), dtype=jnp.int32),
        ),
        "gx",
        0,
    )
    class_sums = gathered_total(owned, GY)
    totals, evidence_sum = (over_axes(group_weights, GX_GY), over_axes(jnp.sum(evidence), GX_GY))
    own_groups = lax.dynamic_slice_in_dim(totals, lax.axis_index("gx"), 1, 0)
    ctf_power = jnp.dot(
        own_groups,
        ctf_table * ctf_table,
        precision=lax.Precision.HIGHEST,
        preferred_element_type=jnp.float32,
    )
    log_evidence = evidence_sum / (rows_here * lax.axis_size("gx") * lax.axis_size(GY) * HALF)
    return (class_sums, ctf_power, log_evidence)


def solution(mesh):
    finer = Mesh(mesh.devices.reshape(mesh.shape["gx"], 4, 4, 2), ("gx", "gy_0", "gy_1", "gy_2"))
    in_specs = (P(GX_GY, None), P("gx", None, None), P(), P(), P(), P(GX_GY), P(), P())
    out_specs = (P("gx", None, None), P("gx", None), P())
    return jax.shard_map(
        shards, mesh=finer, in_specs=in_specs, out_specs=out_specs, check_vma=False
    )
```

profile of v0, /device:TPU:1, one launch (start us, length us, event | category | flops | bytes accessed | tf_op | source)
XLA Modules:
  0.0 449.0 jit_solution(14983572868372554271)
XLA Ops:
  8.1 2.1 reshape.117
  10.2 1.3 convolution_bitcast_fusion.1
  12.5 3.4 fusion.46
  15.9 3.4 fusion.49
  19.9 1.1 copy.47
  21.4 2.0 copy.49
  23.4 1.5 copy.50
  26.2 53.3 %all-gather.5.cloned.1.call-done = bf16[16,12,4096]{2,1,0:T(8,128)(2,1)} async-done(((bf16[1,12,4096]{2,1,0:T(8,128)(2,1)}), bf16[16,12,4096]{2,1,0:T(8,128)(2,1)}) %all-gather.5.cloned.1.call-update) | async-done | bytes 1572880 | tf_op jit(solution)/shard_map/all_gather | solution.py:97
  79.5 60.2 %while.27 = (s32[]{:T(128)}, f32[64,1536]{1,0:T(8,128)S(1)}, bf16[16,12,4096]{2,1,0:T(8,128)(2,1)}, bf16[64,4096]{1,0:T(8,128)(2,1)S(1)}, f32[128,2048]{1,0:T(8,...) while((s32[]{:T(128)}, f32[64,1536]{1,0:T(8,128)S(1)}, ...), condition=%wide.region_1.2_spmd.clone.clone, body=%wide.region_0.1_spmd.clone.clone.sunk | while | flops 92814080 | bytes 4696571 | solution.py:135
  79.6 0.9 bitcast_convert_fusion.2
  83.2 0.9 bitcast_convert_fusion.2
  87.0 0.9 bitcast_convert_fusion.2
  121.0 0.9 bitcast_convert_fusion.2
  140.8 72.5 %while.28 = (s32[]{:T(128)}, f32[16,12,4096]{2,1,0:T(8,128)}, s32[16]{0:T(128)S(1)}, bf16[64,16,96]{0,2,1:T(8,128)(2,1)S(1)}, bf16[64,4096]{1,0:T(8,128)(2,1)S(1...) while((s32[]{:T(128)}, f32[16,12,4096]{2,1,0:T(8,128)}, ...), condition=%wide.region_9.10_spmd.clone.clone, body=%wide.region_6.9_spmd.clone.clone.sunk | while | flops 52166660 | bytes 4629223 | solution.py:175
  213.3 5.5 %copy.54 = f32[16,1,12,4096]{3,1,2,0:T(1,128)S(1)} copy(f32[16,1,12,4096]{3,2,0,1:T(8,128)} %bitcast.10) | data formatting | bytes 6291456 | tf_op jit(solution)/shard_map/reshape | solution.py:20
  218.7 134.6 %all_to_all.5 = f32[16,1,12,4096]{3,1,2,0:T(1,128)S(1)} all-to-all(f32[16,1,12,4096]{3,1,2,0:T(1,128)S(1)} %copy.54), channel_id=1, replica_groups=mesh['gx'=16,'gy_0'=4,'gy_1'=4,'gy_2'=2] {'gx'}, dimensions={0} | all-to-all | bytes 6291456 | tf_op jit(solution)/shard_map/all_to_all | solution.py:25
  353.3 4.3 reduce_sum.86
  358.4 27.7 %all-reduce = (f32[16,128]{1,0:T(8,128)S(1)}, f32[]{:T(128)}) all-reduce(f32[16,128]{1,0:T(8,128)S(1)} %fusion.68, f32[]{:T(128)} %add_reduce_fusion.1), channel_id=1, replica_groups=mesh['gx'=16,'gy_0'=4,'gy_1'=4,'gy_2'=2] {'gx'}, use_global_device_ids=true, to_apply=%region_13.14 | all-reduce | flops 2049 | bytes 16392 | tf_op jit(solution)/shard_map/psum | solution.py:34
  386.1 9.8 %all-reduce.2 = (f32[16,128]{1,0:T(8,128)S(1)}, f32[]{:T(128)}) all-reduce(f32[16,128]{1,0:T(8,128)S(1)} %get-tuple-element.360, f32[]{:T(128)} %get-tuple-element.361), channel_id=1, replica_groups=mesh['gx'=16,'gy_0'=4,'gy_1'=4,'gy_2'=2] {'gy_0'}, use_global_device_ids=true, to_apply=%region_14.15 | all-reduce | flops 2049 | bytes 16392 | tf_op jit(solution)/shard_map/psum | solution.py:34
  395.8 9.3 %all-reduce.1 = (f32[16,128]{1,0:T(8,128)S(1)}, f32[]{:T(128)}) all-reduce(f32[16,128]{1,0:T(8,128)S(1)} %get-tuple-element.364, f32[]{:T(128)} %get-tuple-element.365), channel_id=1, replica_groups=mesh['gx'=16,'gy_0'=4,'gy_1'=4,'gy_2'=2] {'gy_1'}, use_global_device_ids=true, to_apply=%region_15.16 | all-reduce | flops 2049 | bytes 16392 | tf_op jit(solution)/shard_map/psum | solution.py:34
  405.1 25.2 %all-reduce.3 = (f32[16,128]{1,0:T(8,128)S(1)}, f32[]{:T(128)}) all-reduce(f32[16,128]{1,0:T(8,128)S(1)} %get-tuple-element.362, f32[]{:T(128)} %get-tuple-element.363), channel_id=1, replica_groups=mesh['gx'=16,'gy_0'=4,'gy_1'=4,'gy_2'=2] {'gy_2'}, use_global_device_ids=true, to_apply=%region_16.17 | all-reduce | flops 2049 | bytes 16392 | tf_op jit(solution)/shard_map/psum | solution.py:34
  431.0 2.5 fusion.54
  433.4 2.8 all-gather.7.cloned.1.call-done
  436.2 3.9 reduce.5
  (279 shorter events, 103.3 us)
Async XLA Ops:
  7.2 4.3 copy-start.1
  7.2 72.3 %all-gather.5.cloned.1.call-start = ((), (), s32[]{:S(2)}) async-start(), calls=%async_computation.1 | async-start | bytes 2228224 | tf_op jit(solution)/shard_map/all_gather | solution.py:97
  7.9 428.3 %all-gather.7.cloned.1.call-start = ((), (), s32[]{:S(2)}) async-start(), calls=%async_computation.2 | async-start | bytes 8650752 | tf_op jit(solution)/shard_map/all_gather | solution.py:30
  21.3 3.6 copy-start.4
  21.3 3.6 copy-start.5
  21.3 4.0 copy-start.2
  21.3 4.0 copy-start
  21.4 4.0 copy-start.3
Sparse Core Ops, SparseCore 0:
  10.1 69.3 all-gather.4
  357.7 78.4 all-gather.6
where the time goes:
time: 450 us; the launch traced here: 449 us
  blocking collectives  206 us (46%)
  other arithmetic  60.1 us (13%)
  waiting for transfers between devices  56.8 us (13%)
  matrix products  42.2 us (9%)
  local copies, waits for them, and re-layouts  34.8 us (8%)
  loops' own time  32.5 us (7%)
  between operations  16.1 us (4%)
    all_to_all x1, blocking collectives, summed_on_arrival(): lax.all_to_all(tiles, axis, split_axis=0, concat_axis=0, tiled=True)  135 us
    psum x4, blocking collectives, over_axes(): return functools.reduce(lax.psum, axes, shard)  71.9 us
    all_gather x1, waiting for transfers between devices, shards(): piece = lax.all_gather(references, 'gx', axis=0, tiled=True)  53.3 us
    another operation x1, loops' own time, shards(): lax.map(lambda offset: class_terms(offset), jnp.arange(references.shape[0...  31.4 us
    convert_element_type x16, other arithmetic, add_class(): lax.dynamic_index_in_dim(piece, offset, 0, keepdims=False)  14.8 us
    dot_general x16, matrix products, add_class(): jnp.dot(power_table, amplitude.T, precision=lax.Precision.HIGHEST, prefer...  14.7 us
    dynamic_update_slice x16, other arithmetic, shards(): lax.map(lambda offset: class_terms(offset), jnp.arange(references.shape[0...  11.7 us
    cos x32, other arithmetic, phase_tables(): return (jnp.cos(angles), jnp.sin(angles))  11 us
  transfers between devices with their start and end apart: 2, of which 2 were waited for; matrix products, arithmetic and copies ran while one was open for 5% of the time, Pallas kernels for 0%

commit v1 on v0

--- a/solution.py
+++ b/solution.py
@@ -94,7 +94,10 @@
     cosines, sine_table = phase_tables(shift_offsets, L)
     power_table = ctf_table * ctf_table * inv_noise
     blank = jnp.zeros((rows_here, classes * row_width), jnp.float32)
-    piece = lax.all_gather(references, "gx", axis=0, tiled=True)
+    size = lax.axis_size("gx")
+    pieces = jnp.stack([references for _ in range(size)])
+    pieces = lax.all_to_all(pieces, "gx", split_axis=0, concat_axis=0)
+    piece = jnp.concatenate(pieces, axis=0)
 
     def add_class(offset, table):
         stack_row = lax.dynamic_index_in_dim(piece, offset, 0, keepdims=False).astype(jnp.float32)

time: 450 us -> 492 us (1.093)
  waiting for transfers between devices: 56.8 us -> 75.4 us
  starting transfers between devices: 0.08 us -> 16 us
  blocking collectives: 206 us -> 212 us
    all_to_all x0 -> x1, waiting for transfers between devices: none -> 74.4 us  [shards(): pieces = lax.all_to_all(pieces, 'gx', split_axis=0, concat_axis=0)]
    all_gather x1 -> x0, waiting for transfers between devices: 53.3 us -> none  [shards(): piece = lax.all_gather(references, 'gx', axis=0, tiled=True)]
    all_to_all x0 -> x1, starting transfers between devices: none -> 15.9 us  [shards(): pieces = lax.all_to_all(pieces, 'gx', split_axis=0, concat_axis=0)]
    all_to_all x1, blocking collectives: 135 us -> 146 us  [summed_on_arrival(): lax.all_to_all(tiles, axis, split_axis=0, concat_axis=0, tiled=True)]
    psum x4, blocking collectives: 71.9 us -> 66.2 us  [over_axes(): return functools.reduce(lax.psum, axes, shard)]
  transfers between devices with their start and end apart: 2 -> 2, of which waited for: 2 -> 2; matrix products, arithmetic and copies ran while one was open for 5% -> 4% of each run, Pallas kernels for 0% -> 0%
where the time goes in v1:
time: 492 us; the launch traced here: 491 us
  blocking collectives  212 us (43%)
  waiting for transfers between devices  75.4 us (15%)
  other arithmetic  60.1 us (12%)
  matrix products  42.1 us (9%)
  local copies, waits for them, and re-layouts  36.6 us (7%)
  loops' own time  32.5 us (7%)
  between operations  16.1 us (3%)
  starting transfers between devices  16 us (3%)
    all_to_all x1, blocking collectives, summed_on_arrival(): lax.all_to_all(tiles, axis, split_axis=0, concat_axis=0, tiled=True)  146 us
    all_to_all x1, waiting for transfers between devices, shards(): pieces = lax.all_to_all(pieces, 'gx', split_axis=0, concat_axis=0)  74.4 us
    psum x4, blocking collectives, over_axes(): return functools.reduce(lax.psum, axes, shard)  66.2 us
    another operation x1, loops' own time, shards(): lax.map(lambda offset: class_terms(offset), jnp.arange(references.shape[0...  31.4 us
    all_to_all x1, starting transfers between devices, shards(): pieces = lax.all_to_all(pieces, 'gx', split_axis=0, concat_axis=0)  15.9 us
    convert_element_type x16, other arithmetic, add_class(): lax.dynamic_index_in_dim(piece, offset, 0, keepdims=False)  14.8 us
    dot_general x16, matrix products, add_class(): jnp.dot(power_table, amplitude.T, precision=lax.Precision.HIGHEST, prefer...  14.7 us
    dynamic_update_slice x16, other arithmetic, shards(): lax.map(lambda offset: class_terms(offset), jnp.arange(references.shape[0...  11.7 us
  transfers between devices with their start and end apart: 2, of which 2 were waited for; matrix products, arithmetic and copies ran while one was open for 4% of the time, Pallas kernels for 0%

profile of v1, /device:TPU:1, one launch (start us, length us, event | category | flops | bytes accessed | tf_op | source)
XLA Modules:
  0.0 491.1 jit_solution(672126156915585973)
XLA Ops:
  7.2 2.5 stack.2
  9.7 15.9 %all-to-all-start = ((bf16[16,1,12,4096]{3,2,1,0:T(8,128)(2,1)}), bf16[16,1,12,4096]{3,2,1,0:T(8,128)(2,1)}, u32[]{:S(2)}, u32[]{:S(2)}) async-start(bf16[16,1,12,4096]{3,2,1,0:T(8,128)(2,1)} %stack.2), calls=%async_computation | async-start | bytes 4194304 | tf_op jit(solution)/shard_map/all_to_all | solution.py:99
  25.7 1.1 reshape.124
  26.9 1.3 convolution_bitcast_fusion.1
  29.3 3.4 fusion.46
  32.7 3.4 fusion.49
  36.7 1.1 copy.47
  38.1 2.2 copy.49
  40.4 1.5 copy.50
  43.1 74.4 %all-to-all-done = bf16[16,1,12,4096]{3,2,1,0:T(8,128)(2,1)} async-done(((bf16[16,1,12,4096]{3,2,1,0:T(8,128)(2,1)}), bf16[16,1,12,4096]{3,2,1,0:T(8,128)(2,1)}, u32[]{:S(2)}, u32[]{:S(2)}) %all-to-all-start) | async-done | bytes 1572896 | tf_op jit(solution)/shard_map/all_to_all | solution.py:99
  117.5 60.2 %while.27 = (s32[]{:T(128)}, f32[64,1536]{1,0:T(8,128)S(1)}, bf16[16,12,4096]{2,1,0:T(8,128)(2,1)}, bf16[64,4096]{1,0:T(8,128)(2,1)S(1)}, f32[128,2048]{1,0:T(8,...) while((s32[]{:T(128)}, f32[64,1536]{1,0:T(8,128)S(1)}, ...), condition=%wide.region_1.2_spmd.clone.clone, body=%wide.region_0.1_spmd.clone.clone.sunk | while | flops 92814080 | bytes 4696571 | solution.py:138
  117.5 0.9 bitcast_convert_fusion.2
  121.2 0.9 bitcast_convert_fusion.2
  178.8 72.5 %while.28 = (s32[]{:T(128)}, f32[16,12,4096]{2,1,0:T(8,128)}, s32[16]{0:T(128)S(1)}, bf16[64,16,96]{0,2,1:T(8,128)(2,1)S(1)}, bf16[64,4096]{1,0:T(8,128)(2,1)S(1...) while((s32[]{:T(128)}, f32[16,12,4096]{2,1,0:T(8,128)}, ...), condition=%wide.region_9.10_spmd.clone.clone, body=%wide.region_6.9_spmd.clone.clone.sunk | while | flops 52166660 | bytes 4629223 | solution.py:178
  251.3 5.5 %copy.54 = f32[16,1,12,4096]{3,1,2,0:T(1,128)S(1)} copy(f32[16,1,12,4096]{3,2,0,1:T(8,128)} %bitcast.12) | data formatting | bytes 6291456 | tf_op jit(solution)/shard_map/reshape | solution.py:20
  256.7 146.1 %all_to_all.10 = f32[16,1,12,4096]{3,1,2,0:T(1,128)S(1)} all-to-all(f32[16,1,12,4096]{3,1,2,0:T(1,128)S(1)} %copy.54), channel_id=1, replica_groups=mesh['gx'=16,'gy_0'=4,'gy_1'=4,'gy_2'=2] {'gx'}, dimensions={0} | all-to-all | bytes 6291456 | tf_op jit(solution)/shard_map/all_to_all | solution.py:25
  402.9 4.3 reduce_sum.86
  408.0 27.7 %all-reduce = (f32[16,128]{1,0:T(8,128)S(1)}, f32[]{:T(128)}) all-reduce(f32[16,128]{1,0:T(8,128)S(1)} %fusion.68, f32[]{:T(128)} %add_reduce_fusion.1), channel_id=1, replica_groups=mesh['gx'=16,'gy_0'=4,'gy_1'=4,'gy_2'=2] {'gx'}, use_global_device_ids=true, to_apply=%region_13.14 | all-reduce | flops 2049 | bytes 16392 | tf_op jit(solution)/shard_map/psum | solution.py:34
  435.7 10.2 %all-reduce.2 = (f32[16,128]{1,0:T(8,128)S(1)}, f32[]{:T(128)}) all-reduce(f32[16,128]{1,0:T(8,128)S(1)} %get-tuple-element.360, f32[]{:T(128)} %get-tuple-element.361), channel_id=1, replica_groups=mesh['gx'=16,'gy_0'=4,'gy_1'=4,'gy_2'=2] {'gy_0'}, use_global_device_ids=true, to_apply=%region_14.15 | all-reduce | flops 2049 | bytes 16392 | tf_op jit(solution)/shard_map/psum | solution.py:34
  445.9 9.4 %all-reduce.1 = (f32[16,128]{1,0:T(8,128)S(1)}, f32[]{:T(128)}) all-reduce(f32[16,128]{1,0:T(8,128)S(1)} %get-tuple-element.364, f32[]{:T(128)} %get-tuple-element.365), channel_id=1, replica_groups=mesh['gx'=16,'gy_0'=4,'gy_1'=4,'gy_2'=2] {'gy_1'}, use_global_device_ids=true, to_apply=%region_15.16 | all-reduce | flops 2049 | bytes 16392 | tf_op jit(solution)/shard_map/psum | solution.py:34
  455.3 18.9 %all-reduce.3 = (f32[16,128]{1,0:T(8,128)S(1)}, f32[]{:T(128)}) all-reduce(f32[16,128]{1,0:T(8,128)S(1)} %get-tuple-element.362, f32[]{:T(128)} %get-tuple-element.363), channel_id=1, replica_groups=mesh['gx'=16,'gy_0'=4,'gy_1'=4,'gy_2'=2] {'gy_2'}, use_global_device_ids=true, to_apply=%region_16.17 | all-reduce | flops 2049 | bytes 16392 | tf_op jit(solution)/shard_map/psum | solution.py:34
  474.8 2.5 fusion.54
  477.3 1.0 all-gather.4.cloned.1.call-done
  478.3 3.9 reduce.5
  (281 shorter events, 104.3 us)
Async XLA Ops:
  9.7 16.0 %copy-start.1 = (bf16[64,4096]{1,0:T(8,128)(2,1)S(1)}, bf16[64,4096]{1,0:T(8,128)(2,1)}, u32[]{:S(2)}) copy-start(bf16[64,4096]{1,0:T(8,128)(2,1)} %param.12) | copy-start | bytes 1572868
  9.7 107.8 %all-to-all-start = ((bf16[16,1,12,4096]{3,2,1,0:T(8,128)(2,1)}), bf16[16,1,12,4096]{3,2,1,0:T(8,128)(2,1)}, u32[]{:S(2)}, u32[]{:S(2)}) async-start(bf16[16,1,12,4096]{3,2,1,0:T(8,128)(2,1)} %stack.2), calls=%async_computation | async-start | bytes 4194304 | tf_op jit(solution)/shard_map/all_to_all | solution.py:99
  25.6 452.7 %all-gather.4.cloned.1.call-start = ((), (), s32[]{:S(2)}) async-start(), calls=%async_computation.2 | async-start | bytes 8650752 | tf_op jit(solution)/shard_map/all_gather | solution.py:30
  28.3 0.8 copy-start.2
  38.1 3.9 copy-start.5
  38.1 3.9 copy-start.6
  38.1 4.2 copy-start.3
  38.1 4.2 copy-start
  38.1 4.2 copy-start.4
Sparse Core Ops, SparseCore 0:
  407.3 70.9 all-gather.3
